TPU v7x, 32 devices: a whole 2x2x4 slice. The times are simulated.
32 devices in a mesh: dp: 8 (over y, x, core), ctx: 4 (over z).
Axes of the slice: x: 2, y: 2, z: 4, core: 2. Of those that a mesh axis runs over, the one named last changes fastest.
Arguments:
- inputs: bfloat16 [8, 512, 9216], P('dp', 'ctx'), may hold values from -6 to 6
- block_order: int32 [8], replicated, may hold values from 0 to 7, each once
- w_value: bfloat16 [9216, 128], P('dp'), may hold values from -0.0625 to 0.0625
- query: bfloat16 [8, 512, 2048], P('dp', 'ctx'), may hold values from -6 to 6
- keys: bfloat16 [8, 512, 128], P('dp', 'ctx'), may hold values from -6 to 6
- out_grad: bfloat16 [8, 512, 2048], P('dp', 'ctx'), may hold values from -6 to 6
Outputs:
- attn_out: bfloat16 [8, 512, 2048], P('dp', 'ctx')
- grad_query: bfloat16 [8, 512, 2048], P('dp', 'ctx')
- grad_keys: bfloat16 [8, 512, 128], P('dp', 'ctx')
- grad_w: float32 [9216, 128], P('dp')
Inputs may be any that keep to these rules, and one draw needn't show every extreme that they name: `block_order`: a permutation of the block numbers.
All inputs are finite; a program needn't handle non-finite values.
Results may differ from a plain program's by a relative error of at most 0.02.
Values may be sent and summed in bfloat16 or wider, within the bound.
A program may use at most 64 MiB of HBM per device.

v0:
```python
import jax
import jax.numpy as jnp
from jax import lax
from jax.sharding import PartitionSpec as P

BLK = 64


def shifted(value, axis, steps):
    count = lax.axis_size(axis)
    pairs = [(source, (source + steps) % count) for source in range(count)]
    return lax.ppermute(value, axis, pairs)


def shards(inputs, block_order, w_value, query, keys, out_grad):
    x_rows = inputs[0]
    q_rows = query[0]
    k_rows = keys[0]
    grad_rows = out_grad[0]
    rows = x_rows.shape[0]
    head_size = k_rows.shape[1]
    head_count = q_rows.shape[1] // head_size
    scale = 1.0 / head_size**0.5
    values = jnp.dot(
        x_rows,
        lax.all_gather(w_value, "dp", axis=0, tiled=True),
        preferred_element_type=jnp.float32,
    ).astype(jnp.bfloat16)
    far_keys, far_values = shifted((k_rows, values), "ctx", 1)
    index = lax.axis_index("ctx")
    count = lax.axis_size("ctx")
    before = (index + count - 1) % count
    local_iota = jnp.arange(rows, dtype=jnp.int32)

    def places(owner):
        slots = lax.dynamic_slice_in_dim(block_order, 2 * owner, 2, 0)
        return slots[local_iota // BLK] * BLK + local_iota % BLK

    mine = places(index)
    theirs = places(before)
    key_place = jnp.concatenate([mine, theirs], axis=0)
    allowed = key_place[None, :] <= mine[:, None]
    all_keys = jnp.concatenate([k_rows, far_keys], axis=0)
    all_values = jnp.concatenate([values, far_values], axis=0)
    q_flat = q_rows.reshape(rows * head_count, head_size)
    g_flat = grad_rows.reshape(rows * head_count, head_size)
    scores = jnp.dot(q_flat, all_keys.T, preferred_element_type=jnp.float32) * scale
    scores = scores.reshape(rows, head_count, 2 * rows)
    scores = jnp.where(allowed[:, None, :], scores, -1e30)
    top = jnp.max(scores, axis=2, keepdims=True)
    weights = jnp.exp(scores - top)
    prob = (weights / jnp.sum(weights, axis=2, keepdims=True)).reshape(rows * head_count, 2 * rows)
    prob_b = prob.astype(jnp.bfloat16)
    result = jnp.dot(prob_b, all_values, preferred_element_type=jnp.float32).astype(jnp.bfloat16)
    delta = jnp.sum(g_flat.astype(jnp.float32) * result.astype(jnp.float32), axis=1, keepdims=True)
    dprob = jnp.dot(g_flat, all_values.T, preferred_element_type=jnp.float32)
    dscore = (prob * (dprob - delta)).astype(jnp.bfloat16)
    dquery = (jnp.dot(dscore, all_keys, preferred_element_type=jnp.float32) * scale).astype(
        jnp.bfloat16
    )
    dkeys_all = jnp.dot(dscore.T, q_flat, preferred_element_type=jnp.float32) * scale
    dvalues_all = jnp.dot(prob_b.T, g_flat, preferred_element_type=jnp.float32)
    back_keys, back_values = (
        shifted(dkeys_all[rows:].astype(jnp.bfloat16), "ctx", -1).astype(jnp.float32),
        shifted(dvalues_all[rows:].astype(jnp.bfloat16), "ctx", -1).astype(jnp.float32),
    )
    dkeys = (dkeys_all[:rows] + back_keys).astype(jnp.bfloat16)
    dvalues = (dvalues_all[:rows] + back_values).astype(jnp.bfloat16)
    term = jnp.dot(x_rows.T, dvalues, preferred_element_type=jnp.float32)
    partial_sum = lax.psum_scatter(term, "dp", scatter_dimension=0, tiled=True)
    grad_w = lax.psum(partial_sum.astype(jnp.bfloat16), "ctx").astype(jnp.float32)
    attn_rows = result.reshape(rows, head_count * head_size)
    query_grads = dquery.reshape(rows, head_count * head_size)
    return (attn_rows[None], query_grads[None], dkeys[None], grad_w)


def solution(mesh):
    return jax.shard_map(
        shards,
        mesh=mesh,
        in_specs=(
            P("dp", "ctx", None),
            P(),
            P("dp", None),
            P("dp", "ctx", None),
            P("dp", "ctx", None),
            P("dp", "ctx", None),
        ),
        out_specs=(P("dp", "ctx", None), P("dp", "ctx", None), P("dp", "ctx", None), P("dp", None)),
        check_vma=False,
    )
```

profile of v0, /device:TPU:0, one launch (start us, length us, event | category | flops | bytes accessed | tf_op | source)
XLA Modules:
  0.0 145.8 jit_solution(557174618272894783)
XLA Ops:
  8.0 3.1 %collective-permute-start = (bf16[128,128]{1,0:T(8,128)(2,1)}, bf16[128,128]{1,0:T(8,128)(2,1)S(1)}, u32[]{:S(2)}, u32[]{:S(2)}) collective-permute-start(bf16[128,128]{1,0:T(8,128)(2,1)} %bitcast.45), channel_id=1, source_target_pairs={{0,1},{1,2},{2,3},{3,0},{4,5},{5,6},{6,7},{7,4},{8,9},{9,10},{10,1... | collective-permute-start | bytes 98312 | tf_op jit(solution)/shard_map/ppermute | solution.py:12
  12.5 1.3 fusion.24
  13.8 1.3 fusion.21
  16.0 1.0 reshape_squeeze.7
  17.0 1.3 reshape_squeeze.6
  21.2 2.0 %collective-permute-start.3 = (bf16[128,128]{1,0:T(8,128)(2,1)S(1)}, bf16[128,128]{1,0:T(8,128)(2,1)S(1)}, u32[]{:S(2)}, u32[]{:S(2)}) collective-permute-start(bf16[128,128]{1,0:T(8,128)(2,1)S(1)} %slice.39), channel_id=1, source_target_pairs={{0,3},{1,0},{2,1},{3,2},{4,7},{5,4},{6,5},{7,6},{8,11},{9,8},{10,9... | collective-permute-start | bytes 98312 | tf_op jit(solution)/shard_map/ppermute | solution.py:12
  23.2 1.9 %collective-permute-done.3 = bf16[128,128]{1,0:T(8,128)(2,1)S(1)} collective-permute-done((bf16[128,128]{1,0:T(8,128)(2,1)S(1)}, bf16[128,128]{1,0:T(8,128)(2,1)S(1)}, u32[]{:S(2)}, u32[]{:S(2)}) %collective-permute-start.3) | collective-permute-done | bytes 32800 | tf_op jit(solution)/shard_map/ppermute | solution.py:12
  25.1 2.9 %convolution_bitcast_fusion = f32[9216,128]{0,1:T(8,128)} fusion(bf16[1,128,9216]{2,1,0:T(8,128)(2,1)S(1)} %copy-done, f32[256,128]{1,0:T(8,128)S(1)} %fusion.33, bf16[128,128]{1,0:T(8,128)(2,1)S(1)} %collective-permute-done.3), kind=kOutput, calls=%fused_computation | convolution fusion | flops 302039040 | bytes 7176192 | tf_op jit(solution)/shard_map/dot_general | solution.py:69
  28.1 13.5 %all-gather.2.cloned.1.call-done = bf16[9216,128]{1,0:T(8,128)(2,1)} async-done(((bf16[1152,128]{1,0:T(8,128)(2,1)}), bf16[9216,128]{1,0:T(8,128)(2,1)}) %all-gather.2.cloned.1.call-update) | async-done | bytes 2359312 | tf_op jit(solution)/shard_map/all_gather | solution.py:26
  41.7 2.4 %fusion.11 = bf16[128,128]{1,0:T(8,128)(2,1)S(1)} fusion(bf16[9216,128]{1,0:T(8,128)(2,1)} %all-gather.2.cloned.1.call-done, bf16[1,128,9216]{2,1,0:T(8,128)(2,1)S(1)} %copy-done), kind=kOutput, calls=%fused_computation.18 | convolution fusion | flops 302006272 | bytes 4751360 | tf_op jit(solution)/shard_map/dot_general | solution.py:24
  44.1 1.5 %collective-permute-start.1 = (bf16[128,128]{1,0:T(8,128)(2,1)S(1)}, bf16[128,128]{1,0:T(8,128)(2,1)S(1)}, u32[]{:S(2)}, u32[]{:S(2)}) collective-permute-start(bf16[128,128]{1,0:T(8,128)(2,1)S(1)} %fusion.11), channel_id=1, source_target_pairs={{0,1},{1,2},{2,3},{3,0},{4,5},{5,6},{6,7},{7,4},{8,9},{9,10},{10,1... | collective-permute-start | bytes 98312 | tf_op jit(solution)/shard_map/ppermute | solution.py:12
  45.6 2.0 %copy.13 = bf16[2048,128]{0,1:T(8,128)(2,1)} copy(bf16[2048,128]{1,0:T(8,128)(2,1)} %reshape_squeeze.7) | data formatting | bytes 1048576 | tf_op jit(solution)/shard_map/reshape;squeeze | solution.py:46
  47.7 2.2 %collective-permute-done.1 = bf16[128,128]{1,0:T(8,128)(2,1)S(1)} collective-permute-done((bf16[128,128]{1,0:T(8,128)(2,1)S(1)}, bf16[128,128]{1,0:T(8,128)(2,1)S(1)}, u32[]{:S(2)}, u32[]{:S(2)}) %collective-permute-start.1) | collective-permute-done | bytes 32800 | tf_op jit(solution)/shard_map/ppermute | solution.py:12
  49.9 2.3 %multiply_reduce_fusion = (f32[2048]{0:T(1024)S(1)}, bf16[2048,128]{0,1:T(8,128)(2,1)}) fusion(bf16[2048,128]{0,1:T(8,128)(2,1)} %copy.13, bf16[2048,256]{0,1:T(8,128)(2,1)S(1)} %fusion.14, bf16[128,128]{1,0:T(8,128)(2,1)S(1)} %collective-permute-done.1, bf16[128,128]{1,0:T(8,128)(2,1)S(1)} %fusion.11), kind=kOutput, calls=%fused_computation.19 | convolution fusion | flops 135657472 | bytes 2170880 | tf_op jit(solution)/shard_map/dot_general | solution.py:54
  52.1 1.8 %fusion.4 = bf16[2048,256]{0,1:T(8,128)(2,1)S(1)} fusion(bf16[2048,128]{1,0:T(8,128)(2,1)} %reshape_squeeze.7, f32[2048]{0:T(1024)S(1)} %get-tuple-element.20, f32[2048]{0:T(1024)S(1)} %fusion.10, f32[2048,256]{0,1:T(8,128)S(1)} %copy-done.2, f32[2048]{0:T(1024)S(1)} %get-tuple-element.18, bf16[128,128]{1,0:T(8,128)(2,1)S(1)} %collective-permute-done.1, ...), kind=kOutput, calls=%fused_computation.7 | convolution fusion | flops 136970240 | bytes 3760128 | tf_op jit(solution)/shard_map/dot_general | solution.py:56
  55.0 1.4 collective-permute-start.2
  56.4 42.6 %reduce-scatter.2.cloned.1.call-done = f32[1152,128]{0,1:T(8,128)} async-done(((f32[9216,128]{0,1:T(8,128)}), f32[1152,128]{0,1:T(8,128)}) %reduce-scatter.2.cloned.1.call-update) | async-done | bytes 589840 | tf_op jit(solution)/shard_map/reduce_scatter | solution.py:70
  99.0 1.8 %convert_element_type.52 = bf16[1152,128]{0,1:T(8,128)(2,1)} convert(f32[1152,128]{0,1:T(8,128)} %reduce-scatter.2.cloned.1.call-done) | non-fusion elementwise | flops 147456 | bytes 884736 | tf_op jit(solution)/shard_map/convert_element_type | solution.py:71
  100.8 2.1 %fusion.5 = bf16[2048,128]{1,0:T(8,128)(2,1)} fusion(bf16[2048,256]{0,1:T(8,128)(2,1)S(1)} %fusion.4, bf16[128,128]{1,0:T(8,128)(2,1)} %copy-done.8, bf16[128,128]{1,0:T(8,128)(2,1)} %bitcast.46), kind=kOutput, calls=%fused_computation.9 | convolution fusion | flops 134873088 | bytes 1638400 | tf_op jit(solution)/shard_map/dot_general | solution.py:58
  102.9 2.1 %broadcast_in_dim_reshape.7 = bf16[1,128,2048]{2,1,0:T(8,128)(2,1)} reshape(bf16[2048,128]{1,0:T(8,128)(2,1)} %fusion.5) | data formatting | bytes 1048576 | tf_op jit(solution)/shard_map/broadcast_in_dim;reshape | solution.py:74
  105.0 1.3 copy.12
  107.3 1.4 fusion.17
  108.7 28.6 %all-reduce.2.cloned.1.call-done = bf16[1152,128]{0,1:T(8,128)(2,1)} async-done(((bf16[1152,128]{0,1:T(8,128)(2,1)}), bf16[1152,128]{0,1:T(8,128)(2,1)}) %all-reduce.2.cloned.1.call-update) | async-done | bytes 294928 | tf_op jit(solution)/shard_map/psum | solution.py:71
  137.3 1.9 %copy.14 = f32[1152,128]{1,0:T(8,128)} copy(bf16[1152,128]{0,1:T(8,128)(2,1)} %all-reduce.2.cloned.1.call-done) | data formatting | bytes 884736
  (40 shorter events, 8.0 us)
Async XLA Ops:
  7.2 18.0 %copy-start = (bf16[1,128,9216]{2,1,0:T(8,128)(2,1)S(1)}, bf16[1,128,9216]{2,1,0:T(8,128)(2,1)}, u32[]{:S(2)}) copy-start(bf16[1,128,9216]{2,1,0:T(8,128)(2,1)} %param.6) | copy-start | bytes 7077892
  7.2 11.1 %copy-start.7 = (bf16[1,128,128]{2,1,0:T(8,128)(2,1)S(1)}, bf16[1,128,128]{2,1,0:T(8,128)(2,1)}, u32[]{:S(2)}) copy-start(bf16[1,128,128]{2,1,0:T(8,128)(2,1)} %param.10) | copy-start | bytes 98308
  7.2 8.8 %copy-start.6 = (bf16[1,128,2048]{2,1,0:T(8,128)(2,1)S(1)}, bf16[1,128,2048]{2,1,0:T(8,128)(2,1)}, u32[]{:S(2)}) copy-start(bf16[1,128,2048]{2,1,0:T(8,128)(2,1)} %param.11) | copy-start | bytes 1572868
  7.2 34.5 %all-gather.2.cloned.1.call-start = ((), (), s32[]{:S(2)}) async-start(), calls=%async_computation.1 | async-start | bytes 2654208 | tf_op jit(solution)/shard_map/all_gather | solution.py:26
  7.9 91.1 %reduce-scatter.2.cloned.1.call-start = ((), (), s32[]{:S(2)}) async-start(), calls=%async_computation.2 | async-start | bytes 5308416 | tf_op jit(solution)/shard_map/reduce_scatter | solution.py:70
  8.0 10.3 %collective-permute-start = (bf16[128,128]{1,0:T(8,128)(2,1)}, bf16[128,128]{1,0:T(8,128)(2,1)S(1)}, u32[]{:S(2)}, u32[]{:S(2)}) collective-permute-start(bf16[128,128]{1,0:T(8,128)(2,1)} %bitcast.45), channel_id=1, source_target_pairs={{0,1},{1,2},{2,3},{3,0},{4,5},{5,6},{6,7},{7,4},{8,9},{9,10},{10,1... | collective-permute-start | bytes 98312 | tf_op jit(solution)/shard_map/ppermute | solution.py:12
  18.3 0.8 copy-start.3
  18.3 1.1 copy-start.8
  18.9 1.4 copy-start.1
  19.4 1.3 copy-start.5
  21.2 4.0 %collective-permute-start.3 = (bf16[128,128]{1,0:T(8,128)(2,1)S(1)}, bf16[128,128]{1,0:T(8,128)(2,1)S(1)}, u32[]{:S(2)}, u32[]{:S(2)}) collective-permute-start(bf16[128,128]{1,0:T(8,128)(2,1)S(1)} %slice.39), channel_id=1, source_target_pairs={{0,3},{1,0},{2,1},{3,2},{4,7},{5,4},{6,5},{7,6},{8,11},{9,8},{10,9... | collective-permute-start | bytes 98312 | tf_op jit(solution)/shard_map/ppermute | solution.py:12
  28.1 109.2 %all-reduce.2.cloned.1.call-start = ((), (), s32[]{:S(2)}) async-start(), calls=%async_computation.3 | async-start | bytes 589824 | tf_op jit(solution)/shard_map/psum | solution.py:71
  44.1 5.8 %collective-permute-start.1 = (bf16[128,128]{1,0:T(8,128)(2,1)S(1)}, bf16[128,128]{1,0:T(8,128)(2,1)S(1)}, u32[]{:S(2)}, u32[]{:S(2)}) collective-permute-start(bf16[128,128]{1,0:T(8,128)(2,1)S(1)} %fusion.11), channel_id=1, source_target_pairs={{0,1},{1,2},{2,3},{3,0},{4,5},{5,6},{6,7},{7,4},{8,9},{9,10},{10,1... | collective-permute-start | bytes 98312 | tf_op jit(solution)/shard_map/ppermute | solution.py:12
  47.7 4.5 %copy-start.2 = (f32[2048,256]{0,1:T(8,128)S(1)}, f32[2048,256]{0,1:T(8,128)}, u32[]{:S(2)}) copy-start(f32[2048,256]{0,1:T(8,128)} %copy-done.1) | copy-start | bytes 6291460
  52.1 1.8 %copy-start.4 = (bf16[2048,128]{1,0:T(8,128)(2,1)S(1)}, bf16[2048,128]{1,0:T(8,128)(2,1)}, u32[]{:S(2)}) copy-start(bf16[2048,128]{1,0:T(8,128)(2,1)} %copy-done.3) | copy-start | bytes 1572868
  55.0 52.3 %collective-permute-start.2 = (bf16[128,128]{1,0:T(8,128)(2,1)}, bf16[128,128]{1,0:T(8,128)(2,1)}, u32[]{:S(2)}, u32[]{:S(2)}) collective-permute-start(bf16[128,128]{1,0:T(8,128)(2,1)} %slice.40), channel_id=1, source_target_pairs={{0,3},{1,0},{2,1},{3,2},{4,7},{5,4},{6,5},{7,6},{8,11},{9,8},{10,9... | collective-permute-start | bytes 98312 | tf_op jit(solution)/shard_map/ppermute | solution.py:12
Sparse Core Ops, SparseCore 0:
  9.9 31.7 all-gather.1
  45.1 53.8 reduce-scatter.1
  101.5 35.7 all-reduce.1
where the time goes:
time: 147 us; the launch traced here: 146 us
  waiting for transfers between devices  89.6 us (61%)
  local copies, waits for them, and re-layouts  14.7 us (10%)
  between operations  13.9 us (9%)
  matrix products  12.9 us (9%)
  starting transfers between devices  8.15 us (6%)
  other arithmetic  6.52 us (4%)
    reduce_scatter x1, waiting for transfers between devices, shards(): partial_sum = lax.psum_scatter(term, 'dp', scatter_dimension=0, tiled=True)  42.6 us
    psum x1, waiting for transfers between devices, shards(): lax.psum(partial_sum.astype(jnp.bfloat16), 'ctx').astype(jnp.float32)  28.6 us
    all_gather x1, waiting for transfers between devices, shards(): lax.all_gather(w_value, 'dp', axis=0, tiled=True)  13.5 us
    ppermute x4, starting transfers between devices, shifted(): return lax.ppermute(value, axis, pairs)  8.04 us
    ppermute x4, waiting for transfers between devices, shifted(): return lax.ppermute(value, axis, pairs)  4.12 us
    unnamed x19, local copies, waits for them, and re-layouts  3.18 us
    another operation x2, local copies, waits for them, and re-layouts, shards(): return (attn_rows[None], query_grads[None], dkeys[None], grad_w)  3.08 us
    another operation x2, local copies, waits for them, and re-layouts, shards(): g_flat = grad_rows.reshape(rows * head_count, head_size)  3.07 us
  transfers between devices with their start and end apart: 7, of which 5 were waited for; matrix products, arithmetic and copies ran while one was open for 21% of the time, Pallas kernels for 0%

commit v1 on v0

v1 whole, which is shorter than its diff:
```python
import functools

import jax
import jax.numpy as jnp
from jax import lax
from jax.experimental import pallas as pl
from jax.experimental.pallas import tpu as pltpu
from jax.sharding import PartitionSpec as P

MESH = pl.DeviceIdType.MESH
F32 = jnp.float32
BF16 = jnp.bfloat16


def mul16(value):
    return pl.multiple_of(value, 16)


def dot(a, b, ca, cb):
    return lax.dot_general(a, b, (((ca,), (cb,)), ((), ())), preferred_element_type=F32)


def chunk_of(width):
    best = 128
    for size in range(128, 1537, 128):
        if width % size == 0:
            best = size
    return best


def kernel(
    n_dp, n_ctx, group, pieces,
    order, x, w, q, k, g,
    o, dq, dk, gw,
    x2, w_all, k_all, v_all, probs, dv_acc, dk_acc, dvf, dkf, dv2, term, term_r, z_s, z_r, fin,
    send_sem, recv_sem, local_sem,
):
    rows, width = x.shape
    shard, hd = w.shape
    heads = q.shape[1] // hd
    scale = 1.0 / hd**0.5
    chips = n_dp // 2
    aligned = shard % 128 == 0
    me = lax.axis_index("dp")
    z = lax.axis_index("ctx")
    chip, core = me // 2, lax.rem(me, 2)
    sib = me + 1 - 2 * core
    nxt = lax.rem(z + 1, n_ctx)
    prev = lax.rem(z + n_ctx - 1, n_ctx)

    def peer(off):
        return 2 * lax.rem(chip + off, chips) + core

    def source(off):
        return 2 * lax.rem(chip + chips - off, chips) + core

    count = [0]
    sent = []

    def send(src, dst, target):
        at = count[0]
        count[0] += 1
        copy = pltpu.make_async_remote_copy(
            src_ref=src, dst_ref=dst, send_sem=send_sem.at[at], recv_sem=recv_sem.at[at],
            device_id=target, device_id_type=MESH,
        )
        copy.start()
        sent.append(copy)
        return at

    def arrived(ref, at):
        pltpu.make_async_remote_copy(
            src_ref=ref, dst_ref=ref, send_sem=send_sem.at[at], recv_sem=recv_sem.at[at],
            device_id={"dp": sib}, device_id_type=MESH,
        ).wait_recv()

    load = pltpu.make_async_copy(x, x2.at[pl.ds(0, rows)], local_sem)
    load.start()
    k_all[pl.ds(0, rows)] = k[...]

    barrier = pltpu.get_barrier_semaphore()
    for off in range(1, chips):
        pl.semaphore_signal(barrier, inc=1, device_id={"dp": peer(off)}, device_id_type=MESH)
    pl.semaphore_signal(barrier, inc=1, device_id={"dp": sib}, device_id_type=MESH)
    for off in range(1, n_ctx):
        pl.semaphore_signal(
            barrier, inc=1, device_id={"ctx": lax.rem(z + off, n_ctx)}, device_id_type=MESH
        )
    pl.semaphore_wait(barrier, chips + n_ctx - 1)

    keys_at = send(k, k_all.at[pl.ds(rows, rows)], {"ctx": nxt})
    own = pl.ds(mul16(me * shard), shard)
    w_at = [send(w, w_all.at[own], {"dp": peer(off)}) for off in range(1, chips)]
    w_sib_at = [send(w, w_all.at[own], {"dp": sib})]
    x_at = []
    if aligned:
        for j in range(chips):
            cols = pl.ds(pl.multiple_of((2 * j + 1 - core) * shard, 128), shard)
            x_at.append(send(x.at[:, cols], x2.at[pl.ds(rows, rows), cols], {"dp": sib}))
    else:
        x_at.append(send(x, x2.at[pl.ds(rows, rows)], {"dp": sib}))
    w_all[own] = w[...]

    per = order.shape[0] // n_ctx
    blk = rows // per
    span = group * rows
    key_row = lax.broadcasted_iota(jnp.int32, (2 * rows, span), 0)
    q_col = lax.rem(lax.broadcasted_iota(jnp.int32, (2 * rows, span), 1), rows)
    key_place = jnp.zeros((2 * rows, span), jnp.int32)
    q_place = jnp.zeros((2 * rows, span), jnp.int32)
    for b in range(per):
        mine = order[z * per + b]
        theirs = order[prev * per + b]
        key_place = jnp.where(key_row // blk == b, mine * blk + key_row - b * blk, key_place)
        key_place = jnp.where(
            key_row // blk == per + b, theirs * blk + key_row - (per + b) * blk, key_place
        )
        q_place = jnp.where(q_col // blk == b, mine * blk + q_col - b * blk, q_place)
    bias = jnp.where(key_place <= q_place, 0.0, -1e30).astype(F32)

    def stacked(ref, it):
        return jnp.concatenate(
            [
                ref[:, pl.ds(pl.multiple_of((it * group + i) * hd, 128), hd)]
                for i in range(group)
            ],
            axis=0,
        )

    arrived(k_all.at[pl.ds(rows, rows)], keys_at)
    dv_acc[...] = jnp.zeros_like(dv_acc)
    dk_acc[...] = jnp.zeros_like(dk_acc)

    def first(it, carry):
        scores = dot(k_all[...], stacked(q, it), 1, 1) * scale
        scores = jnp.where(bias < 0.0, -1e30, scores)
        top = jnp.max(scores, axis=0, keepdims=True)
        weights = jnp.exp(scores - top)
        prob = weights * (1.0 / jnp.sum(weights, axis=0, keepdims=True))
        probs[it] = prob
        dv_acc[...] += dot(prob.astype(BF16), stacked(g, it), 1, 0)
        return carry

    lax.fori_loop(0, heads // group, first, 0)

    dvf[0] = dv_acc[pl.ds(rows, rows)].astype(BF16)
    at = send(dvf.at[0], dvf.at[1], {"ctx": prev})
    load.wait()
    arrived(dvf.at[1], at)
    dv2[pl.ds(0, rows)] = (dv_acc[pl.ds(0, rows)] + dvf[1].astype(F32)).astype(BF16)
    at = send(dv2.at[pl.ds(0, rows)], dv2.at[pl.ds(rows, rows)], {"dp": sib})
    for j in range(len(x_at)):
        if aligned:
            cols = pl.ds(pl.multiple_of((2 * j + core) * shard, 128), shard)
            arrived(x2.at[pl.ds(rows, rows), cols], x_at[j])
        else:
            arrived(x2.at[pl.ds(rows, rows)], x_at[j])
    arrived(dv2.at[pl.ds(rows, rows)], at)

    def shard_term(index):
        cols = pl.ds(pl.multiple_of(index * shard, 128), shard)
        term[pl.ds(mul16(index * shard), shard)] = dot(x2[:, cols], dv2[...], 0, 0).astype(BF16)

    if aligned:
        for off in range(1, chips):
            shard_term(peer(off))
    else:
        size = chunk_of(width)
        for start in range(0, width, size):
            cols = pl.ds(start, size)
            term[cols] = dot(x2[:, cols], dv2[...], 0, 0).astype(BF16)
    part = shard // pieces

    def piece(step):
        return lax.rem(z + 1 + step, n_ctx) if pieces > 1 else 0

    term_at = []
    for step in range(pieces):
        line = []
        for off in range(1, chips):
            here = pl.ds(mul16(peer(off) * shard + piece(step) * part), part)
            there = pl.ds(mul16(piece(step) * part), part)
            line.append(send(term.at[here], term_r.at[off - 1, there], {"dp": peer(off)}))
        term_at.append(line)
    if aligned:
        shard_term(me)

    for off in range(1, chips):
        came = w_all.at[pl.ds(mul16(source(off) * shard), shard)]
        arrived(came, w_at[off - 1])
        w_sib_at.append(send(came, came, {"dp": sib}))
    for off in range(chips):
        index = source(off) + 1 - 2 * core
        arrived(w_all.at[pl.ds(mul16(index * shard), shard)], w_sib_at[off])
    v_own = pl.ds(0, rows)
    v_far = pl.ds(rows, rows)
    size = chunk_of(width)

    def project(it, total):
        cols = pl.ds(pl.multiple_of(it * size, 128), size)
        return total + dot(x2[pl.ds(0, rows), cols], w_all[cols], 1, 0)

    total = lax.fori_loop(0, width // size, project, jnp.zeros((rows, hd), F32))
    v_all[v_own] = total.astype(BF16)
    at = send(v_all.at[v_own], v_all.at[v_far], {"ctx": nxt})
    arrived(v_all.at[v_far], at)
    v_t = v_all[...].T
    k_t = k_all[...].T

    def second(it, carry):
        prob = probs[it]
        q_rows = stacked(q, it)
        out_t = dot(v_t, prob.astype(BF16), 1, 0)
        dprob = dot(v_all[...], stacked(g, it), 1, 1)
        delta = jnp.sum(prob * dprob, axis=0, keepdims=True)
        dscore = (prob * (dprob - delta)).astype(BF16)
        dk_acc[...] += dot(dscore, q_rows, 1, 0)
        dq_t = dot(k_t, dscore, 1, 0) * scale
        for i in range(group):
            cols = pl.ds(pl.multiple_of((it * group + i) * hd, 128), hd)
            o[:, cols] = out_t[:, i * rows:(i + 1) * rows].T.astype(BF16)
            dq[:, cols] = dq_t[:, i * rows:(i + 1) * rows].T.astype(BF16)
        return carry

    lax.fori_loop(0, heads // group, second, 0)
    dkf[0] = (dk_acc[pl.ds(rows, rows)] * scale).astype(BF16)
    dk_at = send(dkf.at[0], dkf.at[1], {"ctx": prev})

    z_at = []
    for step in range(pieces):
        there = pl.ds(mul16(piece(step) * part), part)
        total = term[pl.ds(mul16(me * shard + piece(step) * part), part)].astype(F32)
        for off in range(1, chips):
            arrived(term_r.at[off - 1, there], term_at[step][off - 1])
            total += term_r[off - 1, there].astype(F32)
        z_s[there] = total.astype(BF16)
        if step < n_ctx - 1 and pieces > 1:
            z_at.append(send(z_s.at[there], z_r.at[z], {"ctx": piece(step)}))
    if pieces == 1:
        for off in range(1, n_ctx):
            z_at.append(send(z_s, z_r.at[z], {"ctx": lax.rem(z + off, n_ctx)}))
    mine = pl.ds(mul16(z * part), part) if pieces > 1 else pl.ds(0, part)
    z_r[z] = z_s[mine]
    arrived(dkf.at[1], dk_at)
    dk[...] = (dk_acc[pl.ds(0, rows)] * scale + dkf[1].astype(F32)).astype(BF16)
    for off in range(1, n_ctx):
        arrived(z_r.at[lax.rem(z + n_ctx - off, n_ctx)], z_at[off - 1])
    total = z_r[0].astype(F32)
    for index in range(1, n_ctx):
        total += z_r[index].astype(F32)
    fin[mine] = total.astype(BF16)
    if pieces > 1:
        f_at = [
            send(fin.at[mine], fin.at[mine], {"ctx": lax.rem(z + off, n_ctx)})
            for off in range(1, n_ctx)
        ]
        for off in range(1, n_ctx):
            index = lax.rem(z + n_ctx - off, n_ctx)
            arrived(fin.at[pl.ds(mul16(index * part), part)], f_at[off - 1])
    gw[...] = fin[...].astype(F32)
    for copy in sent:
        copy.wait_send()


def shards(n_dp, n_ctx, inputs, block_order, w_value, query, keys, out_grad):
    x, q, k, g = inputs[0], query[0], keys[0], out_grad[0]
    rows, width = x.shape
    shard, hd = w_value.shape
    heads = q.shape[1] // hd
    group = 4 if heads % 4 == 0 else 1
    pieces = n_ctx if shard % (16 * n_ctx) == 0 else 1
    part = shard // pieces
    chips = n_dp // 2
    copies = 2 * chips + max(chips, 1) + 8 + (chips - 1) * pieces + 2 * n_ctx
    vmem = pl.BlockSpec(memory_space=pltpu.VMEM)
    o, dq, dk, gw = pl.pallas_call(
        functools.partial(kernel, n_dp, n_ctx, group, pieces),
        out_shape=(
            jax.ShapeDtypeStruct(q.shape, BF16),
            jax.ShapeDtypeStruct(q.shape, BF16),
            jax.ShapeDtypeStruct(k.shape, BF16),
            jax.ShapeDtypeStruct(w_value.shape, F32),
        ),
        in_specs=[
            pl.BlockSpec(memory_space=pltpu.SMEM),
            pl.BlockSpec(memory_space=pl.ANY),
            vmem, vmem, vmem, vmem,
        ],
        out_specs=(vmem, vmem, vmem, vmem),
        scratch_shapes=[
            pltpu.VMEM((2 * rows, width), BF16),
            pltpu.VMEM((width, hd), BF16),
            pltpu.VMEM((2 * rows, hd), BF16),
            pltpu.VMEM((2 * rows, hd), BF16),
            pltpu.VMEM((heads // group, 2 * rows, group * rows), F32),
            pltpu.VMEM((2 * rows, hd), F32),
            pltpu.VMEM((2 * rows, hd), F32),
            pltpu.VMEM((2, rows, hd), BF16),
            pltpu.VMEM((2, rows, hd), BF16),
            pltpu.VMEM((2 * rows, hd), BF16),
            pltpu.VMEM((width, hd), BF16),
            pltpu.VMEM((max(chips - 1, 1), shard, hd), BF16),
            pltpu.VMEM((shard, hd), BF16),
            pltpu.VMEM((n_ctx, part, hd), BF16),
            pltpu.VMEM((shard, hd), BF16),
            pltpu.SemaphoreType.DMA((copies,)),
            pltpu.SemaphoreType.DMA((copies,)),
            pltpu.SemaphoreType.DMA,
        ],
        compiler_params=pltpu.CompilerParams(
            collective_id=0, has_side_effects=True, vmem_limit_bytes=40 * 2**20
        ),
    )(block_order, x, w_value, q, k, g)
    return o[None], dq[None], dk[None], gw


def solution(mesh):
    split = P("dp", "ctx", None)
    return jax.shard_map(
        functools.partial(shards, mesh.shape["dp"], mesh.shape["ctx"]),
        mesh=mesh,
        in_specs=(split, P(), P("dp", None), split, split, split),
        out_specs=(split, split, split, P("dp", None)),
        check_vma=False,
    )
```

time: 147 us -> 55.2 us (0.38)
  waiting for transfers between devices: 89.6 us -> 0 us
  Pallas kernels: 0 us -> 45.1 us
  between operations: 13.9 us -> 0.66 us
  matrix products: 12.9 us -> 0 us
  starting transfers between devices: 8.15 us -> 0 us
  other arithmetic: 6.52 us -> 0 us
  local copies, waits for them, and re-layouts: 14.7 us -> 9.13 us
    pallas_call x0 -> x1, Pallas kernels: none -> 45.1 us  [shards(): pl.pallas_call(functools.partial(kernel, n_dp, n_ctx, group, pieces), out...]
    reduce_scatter x1 -> x0, waiting for transfers between devices: 42.6 us -> none  [shards(): partial_sum = lax.psum_scatter(term, 'dp', scatter_dimension=0, tiled=True)]
    psum x1 -> x0, waiting for transfers between devices: 28.6 us -> none  [shards(): lax.psum(partial_sum.astype(jnp.bfloat16), 'ctx').astype(jnp.float32)]
    all_gather x1 -> x0, waiting for transfers between devices: 13.5 us -> none  [shards(): lax.all_gather(w_value, 'dp', axis=0, tiled=True)]
    dot_general x8 -> x0, matrix products: 12.9 us -> none  [the longest x1 2.94 us: shards(): term = jnp.dot(x_rows.T, dvalues, preferred_element_type=jnp.float32)]
    ppermute x4 -> x0, starting transfers between devices: 8.04 us -> none  [shifted(): return lax.ppermute(value, axis, pairs)]
    another operation x5 -> x0, local copies, waits for them, and re-layouts: 7.44 us -> none  [the longest x2 3.08 us: shards(): return (attn_rows[None], query_grads[None], dkeys[None], grad_w)]
    unnamed x19 -> x16, local copies, waits for them, and re-layouts: 3.18 us -> 9.13 us
  transfers between devices with their start and end apart: 7 -> 0, of which waited for: 5 -> 0; matrix products, arithmetic and copies ran while one was open for 21% -> 0% of each run, Pallas kernels for 0% -> 0%
where the time goes in v1:
time: 55.2 us; the launch traced here: 54.9 us
  Pallas kernels  45.1 us (82%)
  local copies, waits for them, and re-layouts  9.13 us (17%)
  between operations  0.66 us (1%)
    pallas_call x1, Pallas kernels, shards(): pl.pallas_call(functools.partial(kernel, n_dp, n_ctx, group, pieces), out...  45.1 us
    unnamed x16, local copies, waits for them, and re-layouts  9.13 us

profile of v1, /device:TPU:0, one launch (start us, length us, event | category | flops | bytes accessed | tf_op | source)
XLA Modules:
  0.0 54.9 jit_solution(15599330591567177884)
XLA Ops:
  0.6 0.0 copy-start
  0.6 1.7 %copy-done = bf16[1,128,9216]{2,1,0:T(8,128)(2,1)S(1)} copy-done((bf16[1,128,9216]{2,1,0:T(8,128)(2,1)S(1)}, bf16[1,128,9216]{2,1,0:T(8,128)(2,1)}, u32[]{:S(2)}) %copy-start) | copy-done | bytes 2359320
  2.3 0.0 copy-start.1
  2.3 1.0 %copy-done.1 = bf16[1,128,2048]{2,1,0:T(8,128)(2,1)S(1)} copy-done((bf16[1,128,2048]{2,1,0:T(8,128)(2,1)S(1)}, bf16[1,128,2048]{2,1,0:T(8,128)(2,1)}, u32[]{:S(2)}) %copy-start.1) | copy-done | bytes 524312
  3.3 0.0 copy-start.2
  3.3 1.0 %copy-done.2 = bf16[1,128,2048]{2,1,0:T(8,128)(2,1)S(1)} copy-done((bf16[1,128,2048]{2,1,0:T(8,128)(2,1)S(1)}, bf16[1,128,2048]{2,1,0:T(8,128)(2,1)}, u32[]{:S(2)}) %copy-start.2) | copy-done | bytes 524312
  4.4 0.0 copy-start.3
  4.4 1.0 %copy-done.3 = bf16[1152,128]{1,0:T(8,128)(2,1)S(1)} copy-done((bf16[1152,128]{1,0:T(8,128)(2,1)S(1)}, bf16[1152,128]{1,0:T(8,128)(2,1)}, u32[]{:S(2)}) %copy-start.3) | copy-done | bytes 294936
  5.3 0.0 copy-start.4
  5.3 0.8 %copy-done.4 = bf16[1,128,128]{2,1,0:T(8,128)(2,1)S(1)} copy-done((bf16[1,128,128]{2,1,0:T(8,128)(2,1)S(1)}, bf16[1,128,128]{2,1,0:T(8,128)(2,1)}, u32[]{:S(2)}) %copy-start.4) | copy-done | bytes 32792
  6.1 0.0 copy-start.5
  6.1 0.7 %copy-done.5 = s32[8]{0:T(128)S(1)} copy-done((s32[8]{0:T(128)S(1)}, s32[8]{0:T(128)}, u32[]{:S(2)}) %copy-start.5) | copy-done | bytes 56
  6.8 45.1 %shard_map.93 = (bf16[128,2048]{1,0:T(8,128)(2,1)S(1)}, bf16[128,2048]{1,0:T(8,128)(2,1)S(1)}, bf16[128,128]{1,0:T(8,128)(2,1)S(1)}, f32[1152,128]{1,0:T(8,128)S(1)}) custom-call(s32[8]{0:T(128)S(1)} %copy-done.5, bf16[128,9216]{1,0:T(8,128)(2,1)S(1)} %bitcast.7, bf16[1152,128]{1,0:T(8,128)(2,1)S(1)} %copy-done.3, bf16[128,2048]{1,0:T(8,128)(2,1)S(1)} %bitcast.10, ...), custom_call_target="tpu_custom_call" | custom-call | tf_op jit(solution)/shard_map/pallas_call | solution.py:276
  51.8 0.8 %copy.14 = bf16[1,128,2048]{2,1,0:T(8,128)(2,1)} copy(bf16[1,128,2048]{2,1,0:T(8,128)(2,1)S(1)} %bitcast.9) | data formatting | bytes 1048576
  52.6 0.8 %copy.15 = bf16[1,128,2048]{2,1,0:T(8,128)(2,1)} copy(bf16[1,128,2048]{2,1,0:T(8,128)(2,1)S(1)} %bitcast.8) | data formatting | bytes 1048576
  53.4 0.6 %copy.16 = bf16[1,128,128]{2,1,0:T(8,128)(2,1)} copy(bf16[1,128,128]{2,1,0:T(8,128)(2,1)S(1)} %bitcast.13) | data formatting | bytes 65536
  54.0 0.8 %copy.17 = f32[1152,128]{1,0:T(8,128)} copy(f32[1152,128]{1,0:T(8,128)S(1)} %get-tuple-element.19) | data formatting | bytes 1179648
Async XLA Ops:
  0.6 1.7 %copy-start = (bf16[1,128,9216]{2,1,0:T(8,128)(2,1)S(1)}, bf16[1,128,9216]{2,1,0:T(8,128)(2,1)}, u32[]{:S(2)}) copy-start(bf16[1,128,9216]{2,1,0:T(8,128)(2,1)} %param.6) | copy-start | bytes 7077892
  2.3 1.0 %copy-start.1 = (bf16[1,128,2048]{2,1,0:T(8,128)(2,1)S(1)}, bf16[1,128,2048]{2,1,0:T(8,128)(2,1)}, u32[]{:S(2)}) copy-start(bf16[1,128,2048]{2,1,0:T(8,128)(2,1)} %param.9) | copy-start | bytes 1572868
  3.3 1.0 %copy-start.2 = (bf16[1,128,2048]{2,1,0:T(8,128)(2,1)S(1)}, bf16[1,128,2048]{2,1,0:T(8,128)(2,1)}, u32[]{:S(2)}) copy-start(bf16[1,128,2048]{2,1,0:T(8,128)(2,1)} %param.11) | copy-start | bytes 1572868
  4.4 1.0 %copy-start.3 = (bf16[1152,128]{1,0:T(8,128)(2,1)S(1)}, bf16[1152,128]{1,0:T(8,128)(2,1)}, u32[]{:S(2)}) copy-start(bf16[1152,128]{1,0:T(8,128)(2,1)} %w.1) | copy-start | bytes 884740
  5.3 0.8 %copy-start.4 = (bf16[1,128,128]{2,1,0:T(8,128)(2,1)S(1)}, bf16[1,128,128]{2,1,0:T(8,128)(2,1)}, u32[]{:S(2)}) copy-start(bf16[1,128,128]{2,1,0:T(8,128)(2,1)} %param.10) | copy-start | bytes 98308
  6.1 0.7 %copy-start.5 = (s32[8]{0:T(128)S(1)}, s32[8]{0:T(128)}, u32[]{:S(2)}) copy-start(s32[8]{0:T(128)} %order.1) | copy-start | bytes 100

commit v2 on v1

--- a/solution.py
+++ b/solution.py
@@ -29,10 +29,10 @@
 
 
 def kernel(
-    n_dp, n_ctx, group, pieces,
-    order, x, w, q, k, g,
-    o, dq, dk, gw,
-    x2, w_all, k_all, v_all, probs, dv_acc, dk_acc, dvf, dkf, dv2, term, term_r, z_s, z_r, fin,
+    n_dp, n_ctx, group, rounds,
+    order_hbm, x, w, q_hbm, k, g_hbm,
+    o_hbm, dq_hbm, dk_hbm, fin_hbm,
+    o, dq, dk, fin, order, q, g, x2, w_all, k_all, v_all, probs, dv_acc, dk_acc, dvf, dkf, dv2, term, term_r, z_s, z_r,
     send_sem, recv_sem, local_sem,
 ):
     rows, width = x.shape
@@ -40,6 +40,8 @@
     heads = q.shape[1] // hd
     scale = 1.0 / hd**0.5
     chips = n_dp // 2
+    pieces = max(rounds, 1) * (n_ctx if rounds else 1)
+    part = shard // pieces
     aligned = shard % 128 == 0
     me = lax.axis_index("dp")
     z = lax.axis_index("ctx")
@@ -74,9 +76,16 @@
             device_id={"dp": sib}, device_id_type=MESH,
         ).wait_recv()
 
-    load = pltpu.make_async_copy(x, x2.at[pl.ds(0, rows)], local_sem)
-    load.start()
-    k_all[pl.ds(0, rows)] = k[...]
+    own = pl.ds(mul16(me * shard), shard)
+    pairs = [
+        (order_hbm, order), (k, k_all.at[pl.ds(0, rows)]), (q_hbm, q), (g_hbm, g),
+        (x, x2.at[pl.ds(0, rows)]), (w, w_all.at[own]),
+    ]
+    loads = [
+        pltpu.make_async_copy(src, dst, local_sem.at[i]) for i, (src, dst) in enumerate(pairs)
+    ]
+    for load in loads:
+        load.start()
 
     barrier = pltpu.get_barrier_semaphore()
     for off in range(1, chips):
@@ -89,7 +98,6 @@
     pl.semaphore_wait(barrier, chips + n_ctx - 1)
 
     keys_at = send(k, k_all.at[pl.ds(rows, rows)], {"ctx": nxt})
-    own = pl.ds(mul16(me * shard), shard)
     w_at = [send(w, w_all.at[own], {"dp": peer(off)}) for off in range(1, chips)]
     w_sib_at = [send(w, w_all.at[own], {"dp": sib})]
     x_at = []
@@ -99,7 +107,7 @@
             x_at.append(send(x.at[:, cols], x2.at[pl.ds(rows, rows), cols], {"dp": sib}))
     else:
         x_at.append(send(x, x2.at[pl.ds(rows, rows)], {"dp": sib}))
-    w_all[own] = w[...]
+    loads[0].wait()
 
     per = order.shape[0] // n_ctx
     blk = rows // per
@@ -127,6 +135,8 @@
             axis=0,
         )
 
+    for load in loads[1:4]:
+        load.wait()
     arrived(k_all.at[pl.ds(rows, rows)], keys_at)
     dv_acc[...] = jnp.zeros_like(dv_acc)
     dk_acc[...] = jnp.zeros_like(dk_acc)
@@ -145,7 +155,7 @@
 
     dvf[0] = dv_acc[pl.ds(rows, rows)].astype(BF16)
     at = send(dvf.at[0], dvf.at[1], {"ctx": prev})
-    load.wait()
+    loads[4].wait()
     arrived(dvf.at[1], at)
     dv2[pl.ds(0, rows)] = (dv_acc[pl.ds(0, rows)] + dvf[1].astype(F32)).astype(BF16)
     at = send(dv2.at[pl.ds(0, rows)], dv2.at[pl.ds(rows, rows)], {"dp": sib})
@@ -169,22 +179,26 @@
         for start in range(0, width, size):
             cols = pl.ds(start, size)
             term[cols] = dot(x2[:, cols], dv2[...], 0, 0).astype(BF16)
-    part = shard // pieces
-
-    def piece(step):
-        return lax.rem(z + 1 + step, n_ctx) if pieces > 1 else 0
+    def piece(index):
+        if not rounds:
+            return 0
+        return (index // n_ctx) * n_ctx + lax.rem(z + 1 + index % n_ctx, n_ctx)
+
+    def piece_rows(index):
+        return pl.ds(mul16(piece(index) * part), part)
 
     term_at = []
-    for step in range(pieces):
+    for index in range(pieces):
         line = []
         for off in range(1, chips):
-            here = pl.ds(mul16(peer(off) * shard + piece(step) * part), part)
-            there = pl.ds(mul16(piece(step) * part), part)
+            here = pl.ds(mul16(peer(off) * shard + piece(index) * part), part)
+            there = piece_rows(index)
             line.append(send(term.at[here], term_r.at[off - 1, there], {"dp": peer(off)}))
         term_at.append(line)
     if aligned:
         shard_term(me)
 
+    loads[5].wait()
     for off in range(1, chips):
         came = w_all.at[pl.ds(mul16(source(off) * shard), shard)]
         arrived(came, w_at[off - 1])
@@ -203,6 +217,46 @@
     total = lax.fori_loop(0, width // size, project, jnp.zeros((rows, hd), F32))
     v_all[v_own] = total.astype(BF16)
     at = send(v_all.at[v_own], v_all.at[v_far], {"ctx": nxt})
+
+    z_at = []
+
+    def finish_piece(index):
+        there = piece_rows(index)
+        total = term[pl.ds(mul16(me * shard + piece(index) * part), part)].astype(F32)
+        for off in range(1, chips):
+            arrived(term_r.at[off - 1, there], term_at[index][off - 1])
+            total += term_r[off - 1, there].astype(F32)
+        if not rounds:
+            z_s[...] = total.astype(BF16)
+            z_r[0, z] = z_s[...]
+            for off in range(1, n_ctx):
+                z_at.append(send(z_s, z_r.at[0, z], {"ctx": lax.rem(z + off, n_ctx)}))
+            return
+        turn, step = index // n_ctx, index % n_ctx
+        if step < n_ctx - 1:
+            z_s[there] = total.astype(BF16)
+            target = {"ctx": lax.rem(z + 1 + step, n_ctx)}
+            z_at.append(send(z_s.at[there], z_r.at[turn, z], target))
+        else:
+            z_r[turn, z] = total.astype(BF16)
+
+    f_at = []
+
+    def finish_round(turn):
+        for off in range(1, n_ctx):
+            at = z_at[turn * (n_ctx - 1) + off - 1]
+            arrived(z_r.at[turn, lax.rem(z + n_ctx - off, n_ctx)], at)
+        total = z_r[turn, 0].astype(F32)
+        for index in range(1, n_ctx):
+            total += z_r[turn, index].astype(F32)
+        if not rounds:
+            fin[...] = total.astype(BF16)
+            return
+        mine = pl.ds(mul16((turn * n_ctx + z) * part), part)
+        fin[mine] = total.astype(BF16)
+        for off in range(1, n_ctx):
+            f_at.append(send(fin.at[mine], fin.at[mine], {"ctx": lax.rem(z + off, n_ctx)}))
+
     arrived(v_all.at[v_far], at)
     v_t = v_all[...].T
     k_t = k_all[...].T
@@ -222,44 +276,57 @@
             dq[:, cols] = dq_t[:, i * rows:(i + 1) * rows].T.astype(BF16)
         return carry
 
-    lax.fori_loop(0, heads // group, second, 0)
+    steps = heads // group
+    first_round = n_ctx if rounds else 1
+    done = 0
+    for it in range(steps):
+        second(it, 0)
+        upto = first_round * (it + 1) // steps
+        for index in range(done, upto):
+            finish_piece(index)
+        done = upto
+    stores = [
+        pltpu.make_async_copy(src, dst, local_sem.at[i])
+        for i, (src, dst) in enumerate([(o, o_hbm), (dq, dq_hbm), (dk, dk_hbm), (fin, fin_hbm)])
+    ]
+    stores[0].start()
+    stores[1].start()
     dkf[0] = (dk_acc[pl.ds(rows, rows)] * scale).astype(BF16)
     dk_at = send(dkf.at[0], dkf.at[1], {"ctx": prev})
-
-    z_at = []
-    for step in range(pieces):
-        there = pl.ds(mul16(piece(step) * part), part)
-        total = term[pl.ds(mul16(me * shard + piece(step) * part), part)].astype(F32)
-        for off in range(1, chips):
-            arrived(term_r.at[off - 1, there], term_at[step][off - 1])
-            total += term_r[off - 1, there].astype(F32)
-        z_s[there] = total.astype(BF16)
-        if step < n_ctx - 1 and pieces > 1:
-            z_at.append(send(z_s.at[there], z_r.at[z], {"ctx": piece(step)}))
-    if pieces == 1:
-        for off in range(1, n_ctx):
-            z_at.append(send(z_s, z_r.at[z], {"ctx": lax.rem(z + off, n_ctx)}))
-    mine = pl.ds(mul16(z * part), part) if pieces > 1 else pl.ds(0, part)
-    z_r[z] = z_s[mine]
+    finish_round(0)
+    for turn in range(1, rounds):
+        for step in range(n_ctx):
+            finish_piece(turn * n_ctx + step)
     arrived(dkf.at[1], dk_at)
     dk[...] = (dk_acc[pl.ds(0, rows)] * scale + dkf[1].astype(F32)).astype(BF16)
-    for off in range(1, n_ctx):
-        arrived(z_r.at[lax.rem(z + n_ctx - off, n_ctx)], z_at[off - 1])
-    total = z_r[0].astype(F32)
-    for index in range(1, n_ctx):
-        total += z_r[index].astype(F32)
-    fin[mine] = total.astype(BF16)
-    if pieces > 1:
-        f_at = [
-            send(fin.at[mine], fin.at[mine], {"ctx": lax.rem(z + off, n_ctx)})
-            for off in range(1, n_ctx)
-        ]
+    stores[2].start()
+    for turn in range(1, rounds):
+        finish_round(turn)
+    for turn in range(rounds):
         for off in range(1, n_ctx):
-            index = lax.rem(z + n_ctx - off, n_ctx)
-            arrived(fin.at[pl.ds(mul16(index * part), part)], f_at[off - 1])
-    gw[...] = fin[...].astype(F32)
+            index = turn * n_ctx + lax.rem(z + n_ctx - off, n_ctx)
+            theirs = pl.ds(mul16(index * part), part)
+            arrived(fin.at[theirs], f_at[turn * (n_ctx - 1) + off - 1])
+    stores[3].start()
     for copy in sent:
         copy.wait_send()
+    for copy in stores:
+        copy.wait()
+
+
+def finish(o, dq, dk, fin, o_out, dq_out, dk_out, gw, narrow, wide, sem):
+    copies = [
+        pltpu.make_async_copy(src, dst, sem.at[i])
+        for i, (src, dst) in enumerate([(fin, narrow), (o, o_out), (dq, dq_out), (dk, dk_out)])
+    ]
+    for copy in copies:
+        copy.start()
+    copies[0].wait()
+    wide[...] = narrow[...].astype(F32)
+    last = pltpu.make_async_copy(wide, gw, sem.at[4])
+    last.start()
+    for copy in copies[1:] + [last]:
+        copy.wait()
 
 
 def shards(n_dp, n_ctx, inputs, block_order, w_value, query, keys, out_grad):
@@ -268,26 +335,33 @@
     shard, hd = w_value.shape
     heads = q.shape[1] // hd
     group = 4 if heads % 4 == 0 else 1
-    pieces = n_ctx if shard % (16 * n_ctx) == 0 else 1
+    rounds = 0
+    for turns in (1, 2):
+        if shard % (16 * n_ctx * turns) == 0:
+            rounds = turns
+    pieces = max(rounds, 1) * (n_ctx if rounds else 1)
     part = shard // pieces
     chips = n_dp // 2
-    copies = 2 * chips + max(chips, 1) + 8 + (chips - 1) * pieces + 2 * n_ctx
-    vmem = pl.BlockSpec(memory_space=pltpu.VMEM)
-    o, dq, dk, gw = pl.pallas_call(
-        functools.partial(kernel, n_dp, n_ctx, group, pieces),
+    copies = 2 * chips + max(chips, 1) + 8 + (chips - 1) * pieces + 4 * n_ctx
+    hbm = pl.BlockSpec(memory_space=pltpu.HBM)
+    o, dq, dk, fin = pl.pallas_call(
+        functools.partial(kernel, n_dp, n_ctx, group, rounds),
         out_shape=(
             jax.ShapeDtypeStruct(q.shape, BF16),
             jax.ShapeDtypeStruct(q.shape, BF16),
             jax.ShapeDtypeStruct(k.shape, BF16),
-            jax.ShapeDtypeStruct(w_value.shape, F32),
+            jax.ShapeDtypeStruct(w_value.shape, BF16),
         ),
-        in_specs=[
-            pl.BlockSpec(memory_space=pltpu.SMEM),
-            pl.BlockSpec(memory_space=pl.ANY),
-            vmem, vmem, vmem, vmem,
-        ],
-        out_specs=(vmem, vmem, vmem, vmem),
+        in_specs=[hbm] * 6,
+        out_specs=(hbm,) * 4,
         scratch_shapes=[
+            pltpu.VMEM(q.shape, BF16),
+            pltpu.VMEM(q.shape, BF16),
+            pltpu.VMEM(k.shape, BF16),
+            pltpu.VMEM((shard, hd), BF16),
+            pltpu.SMEM(block_order.shape, jnp.int32),
+            pltpu.VMEM(q.shape, BF16),
+            pltpu.VMEM(g.shape, BF16),
             pltpu.VMEM((2 * rows, width), BF16),
             pltpu.VMEM((width, hd), BF16),
             pltpu.VMEM((2 * rows, hd), BF16),
@@ -301,17 +375,32 @@
             pltpu.VMEM((width, hd), BF16),
             pltpu.VMEM((max(chips - 1, 1), shard, hd), BF16),
             pltpu.VMEM((shard, hd), BF16),
-            pltpu.VMEM((n_ctx, part, hd), BF16),
-            pltpu.VMEM((shard, hd), BF16),
+            pltpu.VMEM((max(rounds, 1), n_ctx, part, hd), BF16),
             pltpu.SemaphoreType.DMA((copies,)),
             pltpu.SemaphoreType.DMA((copies,)),
-            pltpu.SemaphoreType.DMA,
+            pltpu.SemaphoreType.DMA((6,)),
         ],
         compiler_params=pltpu.CompilerParams(
-            collective_id=0, has_side_effects=True, vmem_limit_bytes=40 * 2**20
+            collective_id=0, has_side_effects=True, vmem_limit_bytes=60 * 2**20
         ),
     )(block_order, x, w_value, q, k, g)
-    return o[None], dq[None], dk[None], gw
+    return pl.pallas_call(
+        finish,
+        out_shape=(
+            jax.ShapeDtypeStruct(query.shape, BF16),
+            jax.ShapeDtypeStruct(query.shape, BF16),
+            jax.ShapeDtypeStruct(keys.shape, BF16),
+            jax.ShapeDtypeStruct(w_value.shape, F32),
+        ),
+        in_specs=[hbm] * 4,
+        out_specs=(hbm,) * 4,
+        scratch_shapes=[
+            pltpu.VMEM((shard, hd), BF16),
+            pltpu.VMEM((shard, hd), F32),
+            pltpu.SemaphoreType.DMA((5,)),
+        ],
+        compiler_params=pltpu.CompilerParams(vmem_limit_bytes=60 * 2**20),
+    )(o[None], dq[None], dk[None], fin)
 
 
 def solution(mesh):

time: 55.2 us -> 81.7 us (1.48)
  Pallas kernels: 45.1 us -> 80.9 us
  local copies, waits for them, and re-layouts: 9.13 us -> 0 us
    pallas_call x1 -> x2, Pallas kernels: 45.1 us -> 80.9 us  [the longest x1 47 us: shards(): pl.pallas_call(functools.partial(kernel, n_dp, n_ctx, group, rounds), out...]
    unnamed x16 -> x0, local copies, waits for them, and re-layouts: 9.13 us -> none
where the time goes in v2:
time: 81.7 us; the launch traced here: 81.6 us
  Pallas kernels  80.9 us (99%)
    pallas_call x1, Pallas kernels, shards(): pl.pallas_call(functools.partial(kernel, n_dp, n_ctx, group, rounds), out...  47 us
    pallas_call x1, Pallas kernels, shards(): pl.pallas_call(finish, out_shape=(jax.ShapeDtypeStruct(query.shape, BF16)...  33.9 us

profile of v2, /device:TPU:0, one launch (start us, length us, event | category | flops | bytes accessed | tf_op | source)
XLA Modules:
  0.0 81.6 jit_solution(3249436727092538949)
XLA Ops:
  0.6 47.0 %shard_map.93 = (bf16[128,2048]{1,0:T(8,128)(2,1)}, bf16[128,2048]{1,0:T(8,128)(2,1)}, bf16[128,128]{1,0:T(8,128)(2,1)}, bf16[1152,128]{1,0:T(8,128)(2,1)}) custom-call(s32[8]{0:T(128)} %order_hbm.1, bf16[128,9216]{1,0:T(8,128)(2,1)} %bitcast.7, bf16[1152,128]{1,0:T(8,128)(2,1)} %w.1, bf16[128,2048]{1,0:T(8,128)(2,1)} %bitcast.10, ...), custom_call_target="tpu_custom_call" | custom-call | tf_op jit(solution)/shard_map/pallas_call | solution.py:347
  47.7 33.9 %shard_map.94 = (bf16[1,128,2048]{2,1,0:T(8,128)(2,1)}, bf16[1,128,2048]{2,1,0:T(8,128)(2,1)}, bf16[1,128,128]{2,1,0:T(8,128)(2,1)}, f32[1152,128]{1,0:T(8,128)}) custom-call(bf16[1,128,2048]{2,1,0:T(8,128)(2,1)} %bitcast.8, bf16[1,128,2048]{2,1,0:T(8,128)(2,1)} %bitcast.9, bf16[1,128,128]{2,1,0:T(8,128)(2,1)} %bitcast.13, ...), custom_call_target="tpu_custom_call" | custom-call | tf_op jit(solution)/shard_map/pallas_call | solution.py:387

commit v3 on v2

--- a/solution.py
+++ b/solution.py
@@ -28,11 +28,19 @@
     return best
 
 
+def wide_of(chips):
+    best = 1
+    for size in range(1, chips + 1):
+        if size * size <= chips and chips % size == 0:
+            best = size
+    return best
+
+
 def kernel(
     n_dp, n_ctx, group, rounds,
     order_hbm, x, w, q_hbm, k, g_hbm,
     o_hbm, dq_hbm, dk_hbm, fin_hbm,
-    o, dq, dk, fin, order, q, g, x2, w_all, k_all, v_all, probs, dv_acc, dk_acc, dvf, dkf, dv2, term, term_r, z_s, z_r,
+    o, dq, dk, fin, order, q, g, x2, w_all, k_all, v_all, probs, dv_acc, dk_acc, dvf, dkf, dv2, term, term_r, last_s, last_r, z_s, z_r,
     send_sem, recv_sem, local_sem,
 ):
     rows, width = x.shape
@@ -50,11 +58,16 @@
     nxt = lax.rem(z + 1, n_ctx)
     prev = lax.rem(z + n_ctx - 1, n_ctx)
 
-    def peer(off):
-        return 2 * lax.rem(chip + off, chips) + core
-
-    def source(off):
-        return 2 * lax.rem(chip + chips - off, chips) + core
+    wide = wide_of(chips)
+    tall = chips // wide
+    down, across = chip // wide, lax.rem(chip, wide)
+
+    def device(i, j):
+        return 2 * (lax.rem(down + tall + i, tall) * wide + lax.rem(across + wide + j, wide)) + core
+
+    sides = [(0, j) for j in range(1, wide)]
+    heights = [(i, 0) for i in range(1, tall)]
+    others = [(i, j) for i in range(tall) for j in range(wide) if i or j]
 
     count = [0]
     sent = []
@@ -88,18 +101,42 @@
         load.start()
 
     barrier = pltpu.get_barrier_semaphore()
-    for off in range(1, chips):
-        pl.semaphore_signal(barrier, inc=1, device_id={"dp": peer(off)}, device_id_type=MESH)
+    near = sides + heights
+    for i, j in near:
+        pl.semaphore_signal(barrier, inc=1, device_id={"dp": device(i, j)}, device_id_type=MESH)
     pl.semaphore_signal(barrier, inc=1, device_id={"dp": sib}, device_id_type=MESH)
     for off in range(1, n_ctx):
         pl.semaphore_signal(
             barrier, inc=1, device_id={"ctx": lax.rem(z + off, n_ctx)}, device_id_type=MESH
         )
-    pl.semaphore_wait(barrier, chips + n_ctx - 1)
+    pl.semaphore_wait(barrier, len(near) + n_ctx)
 
     keys_at = send(k, k_all.at[pl.ds(rows, rows)], {"ctx": nxt})
-    w_at = [send(w, w_all.at[own], {"dp": peer(off)}) for off in range(1, chips)]
-    w_sib_at = [send(w, w_all.at[own], {"dp": sib})]
+    half = shard // 2 if shard % 32 == 0 else shard
+    halves = [(0, half, sides, heights)]
+    if half < shard:
+        halves.append((half, half, heights, sides))
+
+    def w_rows(index, start, size):
+        return w_all.at[pl.ds(mul16(index * shard + start), size)]
+
+    w_at = {}
+
+    def send_w(start, size, i, j, di, dj):
+        src = w.at[pl.ds(start, size)] if not (i or j) else w_rows(device(-i, -j), start, size)
+        dst = w_rows(device(-i, -j), start, size)
+        w_at[start, i + di, j + dj] = send(src, dst, {"dp": device(di, dj)})
+
+    for start, size, early, late in halves:
+        for i, j in early:
+            send_w(start, size, 0, 0, i, j)
+    for start, size, early, late in halves:
+        for i, j in late:
+            send_w(start, size, 0, 0, i, j)
+    w_sib_at = {}
+    for start, size, early, late in halves:
+        src = w.at[pl.ds(start, size)]
+        w_sib_at[start, 0, 0] = send(src, w_rows(me, start, size), {"dp": sib})
     x_at = []
     if aligned:
         for j in range(chips):
@@ -153,8 +190,20 @@
 
     lax.fori_loop(0, heads // group, first, 0)
 
+    def w_came(start, size, i, j):
+        came = w_rows(device(-i, -j), start, size)
+        arrived(came, w_at[start, i, j])
+        w_sib_at[start, i, j] = send(came, came, {"dp": sib})
+
     dvf[0] = dv_acc[pl.ds(rows, rows)].astype(BF16)
     at = send(dvf.at[0], dvf.at[1], {"ctx": prev})
+    for start, size, early, late in halves:
+        for i, j in early:
+            arrived(w_rows(device(-i, -j), start, size), w_at[start, i, j])
+            for di, dj in late:
+                send_w(start, size, i, j, di, dj)
+            came = w_rows(device(-i, -j), start, size)
+            w_sib_at[start, i, j] = send(came, came, {"dp": sib})
     loads[4].wait()
     arrived(dvf.at[1], at)
     dv2[pl.ds(0, rows)] = (dv_acc[pl.ds(0, rows)] + dvf[1].astype(F32)).astype(BF16)
@@ -172,8 +221,8 @@
         term[pl.ds(mul16(index * shard), shard)] = dot(x2[:, cols], dv2[...], 0, 0).astype(BF16)
 
     if aligned:
-        for off in range(1, chips):
-            shard_term(peer(off))
+        for i, j in others:
+            shard_term(device(i, j))
     else:
         size = chunk_of(width)
         for start in range(0, width, size):
@@ -187,25 +236,54 @@
     def piece_rows(index):
         return pl.ds(mul16(piece(index) * part), part)
 
+    def lanes(index):
+        return (sides, heights) if index % 2 == 0 else (heights, sides)
+
+    def term_rows(index, i, j):
+        return term.at[pl.ds(mul16(device(i, j) * shard + piece(index) * part), part)]
+
     term_at = []
     for index in range(pieces):
-        line = []
-        for off in range(1, chips):
-            here = pl.ds(mul16(peer(off) * shard + piece(index) * part), part)
-            there = piece_rows(index)
-            line.append(send(term.at[here], term_r.at[off - 1, there], {"dp": peer(off)}))
+        early, late = lanes(index)
+        there = piece_rows(index)
+        line = {}
+        for n, (i, j) in enumerate(late + [(0, 0)]):
+            for m, (di, dj) in enumerate(early):
+                line[n, m] = send(
+                    term_rows(index, i + di, j + dj), term_r.at[m, n, there], {"dp": device(di, dj)}
+                )
         term_at.append(line)
     if aligned:
         shard_term(me)
 
+    last_at = []
+
+    def pass_piece(index):
+        early, late = lanes(index)
+        there = piece_rows(index)
+        line = []
+        for n, (i, j) in enumerate(late):
+            total = term_rows(index, i, j)[...].astype(F32)
+            for m in range(len(early)):
+                arrived(term_r.at[m, n, there], term_at[index][n, m])
+                total += term_r[m, n, there].astype(F32)
+            last_s[n, there] = total.astype(BF16)
+            line.append(send(last_s.at[n, there], last_r.at[n, there], {"dp": device(i, j)}))
+        last_at.append(line)
+
     loads[5].wait()
-    for off in range(1, chips):
-        came = w_all.at[pl.ds(mul16(source(off) * shard), shard)]
-        arrived(came, w_at[off - 1])
-        w_sib_at.append(send(came, came, {"dp": sib}))
-    for off in range(chips):
-        index = source(off) + 1 - 2 * core
-        arrived(w_all.at[pl.ds(mul16(index * shard), shard)], w_sib_at[off])
+    for start, size, early, late in halves:
+        for i, j in late:
+            w_came(start, size, i, j)
+        for i, j in others:
+            if i and j:
+                w_came(start, size, i, j)
+    pass_piece(0)
+    if pieces > 1:
+        pass_piece(1)
+    for start, size, early, late in halves:
+        for i, j in [(0, 0)] + others:
+            arrived(w_rows(device(-i, -j) + 1 - 2 * core, start, size), w_sib_at[start, i, j])
     v_own = pl.ds(0, rows)
     v_far = pl.ds(rows, rows)
     size = chunk_of(width)
@@ -223,9 +301,13 @@
     def finish_piece(index):
         there = piece_rows(index)
         total = term[pl.ds(mul16(me * shard + piece(index) * part), part)].astype(F32)
-        for off in range(1, chips):
-            arrived(term_r.at[off - 1, there], term_at[index][off - 1])
-            total += term_r[off - 1, there].astype(F32)
+        early, late = lanes(index)
+        for m in range(len(early)):
+            arrived(term_r.at[m, len(late), there], term_at[index][len(late), m])
+            total += term_r[m, len(late), there].astype(F32)
+        for n in range(len(late)):
+            arrived(last_r.at[n, there], last_at[index][n])
+            total += last_r[n, there].astype(F32)
         if not rounds:
             z_s[...] = total.astype(BF16)
             z_r[0, z] = z_s[...]
@@ -257,6 +339,8 @@
         for off in range(1, n_ctx):
             f_at.append(send(fin.at[mine], fin.at[mine], {"ctx": lax.rem(z + off, n_ctx)}))
 
+    for index in range(2, min(4, pieces)):
+        pass_piece(index)
     arrived(v_all.at[v_far], at)
     v_t = v_all[...].T
     k_t = k_all[...].T
@@ -277,14 +361,20 @@
         return carry
 
     steps = heads // group
-    first_round = n_ctx if rounds else 1
+    jobs = []
+    for index in range(pieces):
+        if index + 4 < pieces:
+            jobs.append(functools.partial(pass_piece, index + 4))
+        jobs.append(functools.partial(finish_piece, index))
+        if index + 1 == n_ctx and rounds:
+            jobs.append(functools.partial(finish_round, 0))
     done = 0
     for it in range(steps):
         second(it, 0)
-        upto = first_round * (it + 1) // steps
-        for index in range(done, upto):
-            finish_piece(index)
-        done = upto
+        upto = 2 * (it + 1) if it + 1 < steps else min(8, len(jobs))
+        for job in jobs[done:upto]:
+            job()
+        done = min(upto, len(jobs))
     stores = [
         pltpu.make_async_copy(src, dst, local_sem.at[i])
         for i, (src, dst) in enumerate([(o, o_hbm), (dq, dq_hbm), (dk, dk_hbm), (fin, fin_hbm)])
@@ -293,10 +383,10 @@
     stores[1].start()
     dkf[0] = (dk_acc[pl.ds(rows, rows)] * scale).astype(BF16)
     dk_at = send(dkf.at[0], dkf.at[1], {"ctx": prev})
-    finish_round(0)
-    for turn in range(1, rounds):
-        for step in range(n_ctx):
-            finish_piece(turn * n_ctx + step)
+    for job in jobs[done:]:
+        job()
+    if not rounds:
+        finish_round(0)
     arrived(dkf.at[1], dk_at)
     dk[...] = (dk_acc[pl.ds(0, rows)] * scale + dkf[1].astype(F32)).astype(BF16)
     stores[2].start()
@@ -314,19 +404,20 @@
         copy.wait()
 
 
-def finish(o, dq, dk, fin, o_out, dq_out, dk_out, gw, narrow, wide, sem):
-    copies = [
-        pltpu.make_async_copy(src, dst, sem.at[i])
-        for i, (src, dst) in enumerate([(fin, narrow), (o, o_out), (dq, dq_out), (dk, dk_out)])
-    ]
-    for copy in copies:
-        copy.start()
-    copies[0].wait()
-    wide[...] = narrow[...].astype(F32)
-    last = pltpu.make_async_copy(wide, gw, sem.at[4])
-    last.start()
-    for copy in copies[1:] + [last]:
-        copy.wait()
+def finish(o, dq, dk, fin, o_out, dq_out, dk_out, gw, o_v, dq_v, dk_v, narrow, wide, sem):
+    ins = [(fin, narrow), (o, o_v), (dq, dq_v), (dk, dk_v)]
+    outs = [(wide, gw), (o_v, o_out), (dq_v, dq_out), (dk_v, dk_out)]
+    loads = [pltpu.make_async_copy(src, dst, sem.at[i]) for i, (src, dst) in enumerate(ins)]
+    stores = [pltpu.make_async_copy(src, dst, sem.at[4 + i]) for i, (src, dst) in enumerate(outs)]
+    for load in loads:
+        load.start()
+    for index in range(4):
+        loads[index].wait()
+        if index == 0:
+            wide[...] = narrow[...].astype(F32)
+        stores[index].start()
+    for store in stores:
+        store.wait()
 
 
 def shards(n_dp, n_ctx, inputs, block_order, w_value, query, keys, out_grad):
@@ -342,7 +433,8 @@
     pieces = max(rounds, 1) * (n_ctx if rounds else 1)
     part = shard // pieces
     chips = n_dp // 2
-    copies = 2 * chips + max(chips, 1) + 8 + (chips - 1) * pieces + 4 * n_ctx
+    most = chips // wide_of(chips)
+    copies = 5 * chips + 16 + 2 * chips * pieces + 4 * n_ctx
     hbm = pl.BlockSpec(memory_space=pltpu.HBM)
     o, dq, dk, fin = pl.pallas_call(
         functools.partial(kernel, n_dp, n_ctx, group, rounds),
@@ -373,7 +465,9 @@
             pltpu.VMEM((2, rows, hd), BF16),
             pltpu.VMEM((2 * rows, hd), BF16),
             pltpu.VMEM((width, hd), BF16),
-            pltpu.VMEM((max(chips - 1, 1), shard, hd), BF16),
+            pltpu.VMEM((most, most, shard, hd), BF16),
+            pltpu.VMEM((most, shard, hd), BF16),
+            pltpu.VMEM((most, shard, hd), BF16),
             pltpu.VMEM((shard, hd), BF16),
             pltpu.VMEM((max(rounds, 1), n_ctx, part, hd), BF16),
             pltpu.SemaphoreType.DMA((copies,)),
@@ -395,9 +489,12 @@
         in_specs=[hbm] * 4,
         out_specs=(hbm,) * 4,
         scratch_shapes=[
+            pltpu.VMEM(query.shape, BF16),
+            pltpu.VMEM(query.shape, BF16),
+            pltpu.VMEM(keys.shape, BF16),
             pltpu.VMEM((shard, hd), BF16),
             pltpu.VMEM((shard, hd), F32),
-            pltpu.SemaphoreType.DMA((5,)),
+            pltpu.SemaphoreType.DMA((8,)),
         ],
         compiler_params=pltpu.CompilerParams(vmem_limit_bytes=60 * 2**20),
     )(o[None], dq[None], dk[None], fin)

time: 81.7 us -> 48.6 us (0.59)
  Pallas kernels: 80.9 us -> 47.8 us
    pallas_call x1, Pallas kernels: 33.9 us -> 2.23 us  [shards(): pl.pallas_call(finish, out_shape=(jax.ShapeDtypeStruct(query.shape, BF16)...]
    pallas_call x1, Pallas kernels: 47 us -> 45.6 us  [shards(): pl.pallas_call(functools.partial(kernel, n_dp, n_ctx, group, rounds), out...]
where the time goes in v3:
time: 48.6 us; the launch traced here: 48.5 us
  Pallas kernels  47.8 us (98%)
  between operations  0.64 us (1%)
    pallas_call x1, Pallas kernels, shards(): pl.pallas_call(functools.partial(kernel, n_dp, n_ctx, group, rounds), out...  45.6 us
    pallas_call x1, Pallas kernels, shards(): pl.pallas_call(finish, out_shape=(jax.ShapeDtypeStruct(query.shape, BF16)...  2.23 us

profile of v3, /device:TPU:0, one launch (start us, length us, event | category | flops | bytes accessed | tf_op | source)
XLA Modules:
  0.0 48.5 jit_solution(12927256535505548989)
XLA Ops:
  0.6 45.6 %shard_map.93 = (bf16[128,2048]{1,0:T(8,128)(2,1)}, bf16[128,2048]{1,0:T(8,128)(2,1)}, bf16[128,128]{1,0:T(8,128)(2,1)}, bf16[1152,128]{1,0:T(8,128)(2,1)}) custom-call(s32[8]{0:T(128)} %order_hbm.1, bf16[128,9216]{1,0:T(8,128)(2,1)} %bitcast.7, bf16[1152,128]{1,0:T(8,128)(2,1)} %w.1, bf16[128,2048]{1,0:T(8,128)(2,1)} %bitcast.10, ...), custom_call_target="tpu_custom_call" | custom-call | tf_op jit(solution)/shard_map/pallas_call | solution.py:439
  46.2 2.2 %shard_map.94 = (bf16[1,128,2048]{2,1,0:T(8,128)(2,1)}, bf16[1,128,2048]{2,1,0:T(8,128)(2,1)}, bf16[1,128,128]{2,1,0:T(8,128)(2,1)}, f32[1152,128]{1,0:T(8,128)}) custom-call(bf16[1,128,2048]{2,1,0:T(8,128)(2,1)} %bitcast.8, bf16[1,128,2048]{2,1,0:T(8,128)(2,1)} %bitcast.9, bf16[1,128,128]{2,1,0:T(8,128)(2,1)} %bitcast.13, ...), custom_call_target="tpu_custom_call" | custom-call | tf_op jit(solution)/shard_map/pallas_call | solution.py:481

commit v4 on v3

--- a/solution.py
+++ b/solution.py
@@ -148,25 +148,24 @@
 
     per = order.shape[0] // n_ctx
     blk = rows // per
-    span = group * rows
-    key_row = lax.broadcasted_iota(jnp.int32, (2 * rows, span), 0)
-    q_col = lax.rem(lax.broadcasted_iota(jnp.int32, (2 * rows, span), 1), rows)
-    key_place = jnp.zeros((2 * rows, span), jnp.int32)
-    q_place = jnp.zeros((2 * rows, span), jnp.int32)
+    key_row = lax.broadcasted_iota(jnp.int32, (2 * rows, rows), 0)
+    q_row = lax.broadcasted_iota(jnp.int32, (2 * rows, rows), 1)
+    key_place = key_row
+    q_place = q_row
     for b in range(per):
         mine = order[z * per + b]
-        theirs = order[prev * per + b]
-        key_place = jnp.where(key_row // blk == b, mine * blk + key_row - b * blk, key_place)
-        key_place = jnp.where(
-            key_row // blk == per + b, theirs * blk + key_row - (per + b) * blk, key_place
-        )
-        q_place = jnp.where(q_col // blk == b, mine * blk + q_col - b * blk, q_place)
-    bias = jnp.where(key_place <= q_place, 0.0, -1e30).astype(F32)
+        q_place = jnp.where(q_row >= b * blk, q_row + (mine - b) * blk, q_place)
+    for b in range(2 * per):
+        owner = z if b < per else prev
+        block = order[owner * per + b % per]
+        key_place = jnp.where(key_row >= b * blk, key_row + (block - b) * blk, key_place)
+    hidden = jnp.where(key_place <= q_place, 0.0, 1.0).astype(F32)
+    hidden = jnp.concatenate([hidden] * group, axis=1)
 
     def stacked(ref, it):
         return jnp.concatenate(
             [
-                ref[:, pl.ds(pl.multiple_of((it * group + i) * hd, 128), hd)]
+                ref[:, pl.ds((it * group + i) * hd, hd)]
                 for i in range(group)
             ],
             axis=0,
@@ -180,7 +179,7 @@
 
     def first(it, carry):
         scores = dot(k_all[...], stacked(q, it), 1, 1) * scale
-        scores = jnp.where(bias < 0.0, -1e30, scores)
+        scores = jnp.where(hidden > 0.0, -1e30, scores)
         top = jnp.max(scores, axis=0, keepdims=True)
         weights = jnp.exp(scores - top)
         prob = weights * (1.0 / jnp.sum(weights, axis=0, keepdims=True))
@@ -188,7 +187,8 @@
         dv_acc[...] += dot(prob.astype(BF16), stacked(g, it), 1, 0)
         return carry
 
-    lax.fori_loop(0, heads // group, first, 0)
+    for it in range(heads // group):
+        first(it, 0)
 
     def w_came(start, size, i, j):
         came = w_rows(device(-i, -j), start, size)
@@ -253,8 +253,6 @@
                     term_rows(index, i + di, j + dj), term_r.at[m, n, there], {"dp": device(di, dj)}
                 )
         term_at.append(line)
-    if aligned:
-        shard_term(me)
 
     last_at = []
 
@@ -278,9 +276,6 @@
         for i, j in others:
             if i and j:
                 w_came(start, size, i, j)
-    pass_piece(0)
-    if pieces > 1:
-        pass_piece(1)
     for start, size, early, late in halves:
         for i, j in [(0, 0)] + others:
             arrived(w_rows(device(-i, -j) + 1 - 2 * core, start, size), w_sib_at[start, i, j])
@@ -288,11 +283,10 @@
     v_far = pl.ds(rows, rows)
     size = chunk_of(width)
 
-    def project(it, total):
-        cols = pl.ds(pl.multiple_of(it * size, 128), size)
-        return total + dot(x2[pl.ds(0, rows), cols], w_all[cols], 1, 0)
-
-    total = lax.fori_loop(0, width // size, project, jnp.zeros((rows, hd), F32))
+    total = jnp.zeros((rows, hd), F32)
+    for start in range(0, width, size):
+        cols = pl.ds(start, size)
+        total = total + dot(x2[pl.ds(0, rows), cols], w_all[cols], 1, 0)
     v_all[v_own] = total.astype(BF16)
     at = send(v_all.at[v_own], v_all.at[v_far], {"ctx": nxt})
 
@@ -339,7 +333,9 @@
         for off in range(1, n_ctx):
             f_at.append(send(fin.at[mine], fin.at[mine], {"ctx": lax.rem(z + off, n_ctx)}))
 
-    for index in range(2, min(4, pieces)):
+    if aligned:
+        shard_term(me)
+    for index in range(min(4, pieces)):
         pass_piece(index)
     arrived(v_all.at[v_far], at)
     v_t = v_all[...].T
@@ -355,9 +351,9 @@
         dk_acc[...] += dot(dscore, q_rows, 1, 0)
         dq_t = dot(k_t, dscore, 1, 0) * scale
         for i in range(group):
-            cols = pl.ds(pl.multiple_of((it * group + i) * hd, 128), hd)
-            o[:, cols] = out_t[:, i * rows:(i + 1) * rows].T.astype(BF16)
-            dq[:, cols] = dq_t[:, i * rows:(i + 1) * rows].T.astype(BF16)
+            cols = pl.ds((it * group + i) * hd, hd)
+            o[:, cols] = out_t[:, i * rows:(i + 1) * rows].astype(BF16).T
+            dq[:, cols] = dq_t[:, i * rows:(i + 1) * rows].astype(BF16).T
         return carry
 
     steps = heads // group

time: 48.6 us -> 47.8 us (0.984)
  Pallas kernels: 47.8 us -> 47.1 us
    pallas_call x1, Pallas kernels: 45.6 us -> 44.8 us  [shards(): pl.pallas_call(functools.partial(kernel, n_dp, n_ctx, group, rounds), out...]
where the time goes in v4:
time: 47.8 us; the launch traced here: 47.7 us
  Pallas kernels  47.1 us (99%)
  between operations  0.64 us (1%)
    pallas_call x1, Pallas kernels, shards(): pl.pallas_call(functools.partial(kernel, n_dp, n_ctx, group, rounds), out...  44.8 us
    pallas_call x1, Pallas kernels, shards(): pl.pallas_call(finish, out_shape=(jax.ShapeDtypeStruct(query.shape, BF16)...  2.23 us

profile of v4, /device:TPU:0, one launch (start us, length us, event | category | flops | bytes accessed | tf_op | source)
XLA Modules:
  0.0 47.7 jit_solution(5182919431164588159)
XLA Ops:
  0.6 44.8 %shard_map.93 = (bf16[128,2048]{1,0:T(8,128)(2,1)}, bf16[128,2048]{1,0:T(8,128)(2,1)}, bf16[128,128]{1,0:T(8,128)(2,1)}, bf16[1152,128]{1,0:T(8,128)(2,1)}) custom-call(s32[8]{0:T(128)} %order_hbm.1, bf16[128,9216]{1,0:T(8,128)(2,1)} %bitcast.7, bf16[1152,128]{1,0:T(8,128)(2,1)} %w.1, bf16[128,2048]{1,0:T(8,128)(2,1)} %bitcast.10, ...), custom_call_target="tpu_custom_call" | custom-call | tf_op jit(solution)/shard_map/pallas_call | solution.py:435
  45.5 2.2 %shard_map.94 = (bf16[1,128,2048]{2,1,0:T(8,128)(2,1)}, bf16[1,128,2048]{2,1,0:T(8,128)(2,1)}, bf16[1,128,128]{2,1,0:T(8,128)(2,1)}, f32[1152,128]{1,0:T(8,128)}) custom-call(bf16[1,128,2048]{2,1,0:T(8,128)(2,1)} %bitcast.8, bf16[1,128,2048]{2,1,0:T(8,128)(2,1)} %bitcast.9, bf16[1,128,128]{2,1,0:T(8,128)(2,1)} %bitcast.13, ...), custom_call_target="tpu_custom_call" | custom-call | tf_op jit(solution)/shard_map/pallas_call | solution.py:477

commit v5 on v4

--- a/solution.py
+++ b/solution.py
@@ -40,7 +40,7 @@
     n_dp, n_ctx, group, rounds,
     order_hbm, x, w, q_hbm, k, g_hbm,
     o_hbm, dq_hbm, dk_hbm, fin_hbm,
-    o, dq, dk, fin, order, q, g, x2, w_all, k_all, v_all, probs, dv_acc, dk_acc, dvf, dkf, dv2, term, term_r, last_s, last_r, z_s, z_r,
+    o, dq, dk, fin, order, q, g, x2, w_all, k_all, v_all, probs, dv_acc, dv_sib, dk_acc, dvf, dkf, dv2, term, term_r, last_s, last_r, z_s, z_r,
     send_sem, recv_sem, local_sem,
 ):
     rows, width = x.shape
@@ -109,7 +109,9 @@
         pl.semaphore_signal(
             barrier, inc=1, device_id={"ctx": lax.rem(z + off, n_ctx)}, device_id_type=MESH
         )
-    pl.semaphore_wait(barrier, len(near) + n_ctx)
+    pl.semaphore_signal(barrier, inc=1, device_id={"dp": sib, "ctx": nxt}, device_id_type=MESH)
+    pl.semaphore_signal(barrier, inc=1, device_id={"dp": sib, "ctx": prev}, device_id_type=MESH)
+    pl.semaphore_wait(barrier, len(near) + n_ctx + 2)
 
     keys_at = send(k, k_all.at[pl.ds(rows, rows)], {"ctx": nxt})
     half = shard // 2 if shard % 32 == 0 else shard
@@ -197,6 +199,8 @@
 
     dvf[0] = dv_acc[pl.ds(rows, rows)].astype(BF16)
     at = send(dvf.at[0], dvf.at[1], {"ctx": prev})
+    sib_far_at = send(dvf.at[0], dvf.at[2], {"dp": sib, "ctx": prev})
+    sib_own_at = send(dv_acc.at[pl.ds(0, rows)], dv_sib, {"dp": sib})
     for start, size, early, late in halves:
         for i, j in early:
             arrived(w_rows(device(-i, -j), start, size), w_at[start, i, j])
@@ -207,14 +211,15 @@
     loads[4].wait()
     arrived(dvf.at[1], at)
     dv2[pl.ds(0, rows)] = (dv_acc[pl.ds(0, rows)] + dvf[1].astype(F32)).astype(BF16)
-    at = send(dv2.at[pl.ds(0, rows)], dv2.at[pl.ds(rows, rows)], {"dp": sib})
     for j in range(len(x_at)):
         if aligned:
             cols = pl.ds(pl.multiple_of((2 * j + core) * shard, 128), shard)
             arrived(x2.at[pl.ds(rows, rows), cols], x_at[j])
         else:
             arrived(x2.at[pl.ds(rows, rows)], x_at[j])
-    arrived(dv2.at[pl.ds(rows, rows)], at)
+    arrived(dv_sib, sib_own_at)
+    arrived(dvf.at[2], sib_far_at)
+    dv2[pl.ds(rows, rows)] = (dv_sib[...] + dvf[2].astype(F32)).astype(BF16)
 
     def shard_term(index):
         cols = pl.ds(pl.multiple_of(index * shard, 128), shard)
@@ -357,17 +362,15 @@
         return carry
 
     steps = heads // group
-    jobs = []
+    jobs = [functools.partial(pass_piece, index) for index in range(4, pieces)]
     for index in range(pieces):
-        if index + 4 < pieces:
-            jobs.append(functools.partial(pass_piece, index + 4))
         jobs.append(functools.partial(finish_piece, index))
         if index + 1 == n_ctx and rounds:
             jobs.append(functools.partial(finish_round, 0))
     done = 0
     for it in range(steps):
         second(it, 0)
-        upto = 2 * (it + 1) if it + 1 < steps else min(8, len(jobs))
+        upto = 3 * (it + 1)
         for job in jobs[done:upto]:
             job()
         done = min(upto, len(jobs))
@@ -456,8 +459,9 @@
             pltpu.VMEM((2 * rows, hd), BF16),
             pltpu.VMEM((heads // group, 2 * rows, group * rows), F32),
             pltpu.VMEM((2 * rows, hd), F32),
+            pltpu.VMEM((rows, hd), F32),
             pltpu.VMEM((2 * rows, hd), F32),
-            pltpu.VMEM((2, rows, hd), BF16),
+            pltpu.VMEM((3, rows, hd), BF16),
             pltpu.VMEM((2, rows, hd), BF16),
             pltpu.VMEM((2 * rows, hd), BF16),
             pltpu.VMEM((width, hd), BF16),

time: 47.8 us -> 47.8 us (level)
  no operation moved by 1% of the time
where the time goes in v5:
time: 47.8 us; the launch traced here: 47.7 us
  Pallas kernels  47 us (98%)
  between operations  0.64 us (1%)
    pallas_call x1, Pallas kernels, shards(): pl.pallas_call(functools.partial(kernel, n_dp, n_ctx, group, rounds), out...  44.8 us
    pallas_call x1, Pallas kernels, shards(): pl.pallas_call(finish, out_shape=(jax.ShapeDtypeStruct(query.shape, BF16)...  2.23 us

profile of v5, /device:TPU:0, one launch (start us, length us, event | category | flops | bytes accessed | tf_op | source)
XLA Modules:
  0.0 47.7 jit_solution(3306591614542202118)
XLA Ops:
  0.6 44.8 %shard_map.93 = (bf16[128,2048]{1,0:T(8,128)(2,1)}, bf16[128,2048]{1,0:T(8,128)(2,1)}, bf16[128,128]{1,0:T(8,128)(2,1)}, bf16[1152,128]{1,0:T(8,128)(2,1)}) custom-call(s32[8]{0:T(128)} %order_hbm.1, bf16[128,9216]{1,0:T(8,128)(2,1)} %bitcast.7, bf16[1152,128]{1,0:T(8,128)(2,1)} %w.1, bf16[128,2048]{1,0:T(8,128)(2,1)} %bitcast.10, ...), custom_call_target="tpu_custom_call" | custom-call | tf_op jit(solution)/shard_map/pallas_call | solution.py:438
  45.5 2.2 %shard_map.94 = (bf16[1,128,2048]{2,1,0:T(8,128)(2,1)}, bf16[1,128,2048]{2,1,0:T(8,128)(2,1)}, bf16[1,128,128]{2,1,0:T(8,128)(2,1)}, f32[1152,128]{1,0:T(8,128)}) custom-call(bf16[1,128,2048]{2,1,0:T(8,128)(2,1)} %bitcast.8, bf16[1,128,2048]{2,1,0:T(8,128)(2,1)} %bitcast.9, bf16[1,128,128]{2,1,0:T(8,128)(2,1)} %bitcast.13, ...), custom_call_target="tpu_custom_call" | custom-call | tf_op jit(solution)/shard_map/pallas_call | solution.py:481
